TPU v7x, 32 devices: a whole 2x2x4 slice. The times are simulated.
32 devices in a mesh: groups: 2 (over x), wide: 16 (over z, y, core).
Axes of the slice: x: 2, y: 2, z: 4, core: 2. Of those that a mesh axis runs over, the one named last changes fastest.
Arguments:
- doc_len: int32 [256], P('groups'), parts along dimension 0, may hold values from 1 to 505, as said below
- doc_owner: int32 [256], P('groups'), parts along dimension 0, may hold values from 0 to 127, each once
- query_act: bfloat16 [256, 4096], P('groups'), parts along dimension 0, may hold values from -0.09375 to 0.09375
- query_grad: bfloat16 [256, 7168], P('groups'), parts along dimension 0, may hold values from -0.0625 to 0.0625
- basis_act: bfloat16 [8192, 4096], P('groups', 'wide'), parts along dimension 0, may hold values from -0.09375 to 0.09375
- basis_grad: bfloat16 [14336, 7168], P('groups', 'wide'), parts along dimension 0, may hold values from -0.0625 to 0.0625
- eig_act: float32 [8192], P(('groups', 'wide')), parts along dimension 0, may hold values from 0.02 to 5
- eig_grad: float32 [14336], P(('groups', 'wide')), parts along dimension 0, may hold values from 0.02 to 5
- token_act: bfloat16 [16384, 4096], P(('groups', 'wide')), parts along dimension 0, may hold values from -6 to 6
- token_grad: bfloat16 [16384, 7168], P(('groups', 'wide')), parts along dimension 0, may hold values from -6 to 6
Outputs:
- scores: float32 [256, 64], P(('groups', 'wide')), parts along dimension 0
There are 2 independent parts, one for each index of `groups`. A program takes and returns all parts, laid end to end along the dimension named above; each array names one. Nothing has to cross between parts.
Inputs may be any that keep to these rules, and one draw needn't show every extreme that they name: `doc_len`: each device's 8 lengths are at least 1 and sum to 16 times a whole number from 1 to 32; the devices' sums add up to 4224, and on some device the sum is 512, with one document of 505 rows.
All inputs are finite; a program needn't handle non-finite values.
Results may differ from a plain program's by a relative error of at most 0.0003.
Values may be sent and summed in bfloat16 or wider, within the bound.
A program may use at most 128 MiB of HBM per device.

v0:
```python
import jax
import jax.numpy as jnp
from jax import lax
from jax.sharding import PartitionSpec as P

RANK = 2


DAMP = 0.1


def owners_and_weights(doc_len, doc_owner, width, source, place):
    docs = doc_len.shape[0] // width
    ends = jnp.cumsum(doc_len.reshape(width, docs), axis=1)
    picked = (source[:, None] == jnp.arange(width)[None, :]).astype(jnp.int32)
    row_ends = jnp.sum(picked[:, :, None] * ends[None, :, :], axis=1)
    live = place < row_ends[:, docs - 1]
    within = jnp.minimum(jnp.sum((place[:, None] >= row_ends).astype(jnp.int32), axis=1), docs - 1)
    global_doc = source * docs + within
    matches = (global_doc[:, None] == jnp.arange(doc_len.shape[0])[None, :]).astype(jnp.int32)
    length = jnp.sum(matches * doc_len[None, :], axis=1).astype(jnp.float32)
    owner = jnp.sum(matches * doc_owner[None, :], axis=1)
    weight = jnp.where(live, 1.0 / length, jnp.float32(0.0))
    return (owner, weight)


def pair_products(hat, tok_act, tok_grad, width_act):
    inner = (((1,), (1,)), ((), ()))
    prod_act = lax.dot_general(
        hat[:, :width_act],
        tok_act,
        inner,
        precision=lax.Precision.HIGHEST,
        preferred_element_type=jnp.float32,
    )
    prod_grad = lax.dot_general(
        hat[:, width_act:],
        tok_grad,
        inner,
        precision=lax.Precision.HIGHEST,
        preferred_element_type=jnp.float32,
    )
    return prod_act * prod_grad


def shards(
    doc_len,
    doc_owner,
    query_act,
    query_grad,
    basis_act,
    basis_grad,
    eig_act,
    eig_grad,
    token_act,
    token_grad,
):
    width = lax.axis_size("wide")
    myself = lax.axis_index("wide")
    width_act = query_act.shape[1]
    qrows = query_act.shape[0]
    scale_act = 1.0 / (eig_act + DAMP)
    scale_grad = 1.0 / (eig_grad + DAMP)
    back = (((1,), (1,)), ((), ()))
    wide_basis_act = basis_act.astype(jnp.float32)
    wide_basis_grad = basis_grad.astype(jnp.float32)
    tok_rows = token_act.shape[0]
    tok_act = token_act
    tok_grad = token_grad
    source = jnp.zeros((tok_rows,), jnp.int32) + myself
    place = jnp.arange(tok_rows)
    owner, weight = owners_and_weights(doc_len, doc_owner, width, source, place)
    tok_act = tok_act.astype(jnp.float32)
    tok_grad = tok_grad.astype(jnp.float32)
    coords_act = jnp.dot(query_act, basis_act, preferred_element_type=jnp.float32) * scale_act
    coords_grad = jnp.dot(query_grad, basis_grad, preferred_element_type=jnp.float32) * scale_grad
    part_act = lax.dot_general(
        coords_act,
        wide_basis_act,
        back,
        precision=lax.Precision.HIGHEST,
        preferred_element_type=jnp.float32,
    )
    part_grad = lax.dot_general(
        coords_grad,
        wide_basis_grad,
        back,
        precision=lax.Precision.HIGHEST,
        preferred_element_type=jnp.float32,
    )
    hat = lax.psum(jnp.concatenate([part_act, part_grad], axis=1), "wide")
    products = pair_products(hat, tok_act, tok_grad, width_act)
    scores_tok = products.reshape(qrows // RANK, RANK, products.shape[1]).sum(axis=1)
    column = jnp.arange(doc_len.shape[0] // width * lax.axis_size("wide"))
    member = (owner[:, None] == column[None, :]).astype(jnp.float32) * weight[:, None]
    return lax.psum_scatter(
        lax.dot_general(
            member,
            scores_tok,
            (((0,), (1,)), ((), ())),
            precision=lax.Precision.HIGHEST,
            preferred_element_type=jnp.float32,
        ),
        "wide",
        scatter_dimension=0,
        tiled=True,
    )


def solution(mesh):
    placed = (
        P("groups"),
        P("groups"),
        P("groups", None),
        P("groups", None),
        P("groups", "wide"),
        P("groups", "wide"),
        P(("groups", "wide")),
        P(("groups", "wide")),
        P(("groups", "wide"), None),
        P(("groups", "wide"), None),
    )
    return jax.shard_map(
        shards, mesh=mesh, in_specs=placed, out_specs=P(("groups", "wide"), None), check_vma=False
    )
```

profile of v0, /device:TPU:0, one launch (start us, length us, event | category | flops | bytes accessed | tf_op | source)
XLA Modules:
  0.0 242.8 jit_solution(15273020945481043469)
XLA Ops:
  6.5 0.0 copy-start
  6.5 0.8 add_divide_fusion
  7.4 5.6 %convolution_multiply_fusion = f32[128,448]{0,1:T(8,128)S(1)} fusion(bf16[128,7168]{1,0:T(8,128)(2,1)} %param.13, bf16[7168,448]{0,1:T(8,128)(2,1)} %param.15, f32[448]{0:T(512)S(1)} %add_divide_fusion), kind=kOutput, calls=%fused_computation.6 | convolution fusion | flops 822140928 | bytes 8488704 | tf_op jit(solution)/shard_map/dot_general | solution.py:76
  13.0 0.0 copy-start.4
  13.0 0.0 copy-start.2
  13.0 3.3 %fusion.14 = f32[128,7168]{1,0:T(8,128)S(1)} fusion(f32[128,448]{0,1:T(8,128)S(1)} %convolution_multiply_fusion, bf16[7168,448]{0,1:T(8,128)(2,1)S(1)} %bitcast.15), kind=kOutput, calls=%fused_computation.29 | convolution fusion | flops 4932501504 | bytes 10321920 | tf_op jit(solution)/shard_map/dot_general | solution.py:84
  16.4 0.5 convolution_multiply_fusion.1
  16.9 2.2 fusion.13
  19.0 3.0 %pad_maximum_fusion = f32[128,11264]{1,0:T(8,128)} fusion(f32[128,7168]{1,0:T(8,128)S(1)} %fusion.14, f32[128,4096]{1,0:T(8,128)S(1)} %fusion.13), kind=kLoop, calls=%fused_computation | loop fusion | flops 1441792 | bytes 11534336 | tf_op jit(solution)/shard_map/concatenate | solution.py:91
  22.0 0.0 all-reduce.3.cloned.1.call-update
  22.0 0.6 copy-done.3
  22.7 0.1 reduce_window_sum.13
  22.7 0.2 reduce_window_sum.14
  22.9 0.6 dynamic-slice
  24.2 0.1 multiply_reduce_fusion
  24.3 0.3 select_reduce_fusion.1
  24.6 132.3 %all-reduce.3.cloned.1.call-done = f32[128,11264]{1,0:T(8,128)} async-done(((f32[128,11264]{1,0:T(8,128)}), f32[128,11264]{1,0:T(8,128)}) %all-reduce.3.cloned.1.call-update) | async-done | bytes 5767184 | tf_op jit(solution)/shard_map/psum | solution.py:91
  156.9 11.1 %fusion = f32[128,512]{1,0:T(8,128)S(1)} fusion(bf16[512,7168]{1,0:T(8,128)(2,1)} %param.19, f32[128,11264]{1,0:T(8,128)} %all-reduce.3.cloned.1.call-done), kind=kOutput, calls=%fused_computation.1 | convolution fusion | flops 5637144576 | bytes 11272192 | tf_op jit(solution)/shard_map/dot_general | solution.py:36
  168.0 5.8 %fusion.4 = f32[128,512]{1,0:T(8,128)S(1)} fusion(f32[128,512]{1,0:T(8,128)S(1)} %fusion, bf16[512,4096]{1,0:T(8,128)(2,1)S(1)} %copy-done.1, f32[128,11264]{1,0:T(8,128)} %all-reduce.3.cloned.1.call-done), kind=kOutput, calls=%fused_computation.5 | convolution fusion | flops 3221291008 | bytes 6815744 | tf_op jit(solution)/shard_map/dot_general | solution.py:29
  173.8 0.1 reshape.43
  174.0 0.3 reduce_sum.49
  174.3 0.7 fusion.7
  175.0 60.4 %all-reduce = f32[128,64]{1,0:T(8,128)S(1)} all-reduce(f32[128,64]{1,0:T(8,128)S(1)} %fusion.7), channel_id=2, replica_groups=mesh['groups'=2,'wide'=16] {'wide'}, use_global_device_ids=true, to_apply=%region_7.8.clone | all-reduce | flops 8192 | bytes 65536
  235.4 0.6 constant_dynamic-slice_fusion
  (22 shorter events, 0.1 us)
Async XLA Ops:
  6.5 9.8 %copy-start = (bf16[4096,256]{1,0:T(8,128)(2,1)S(1)}, bf16[4096,256]{1,0:T(8,128)(2,1)}, u32[]{:S(2)}) copy-start(bf16[4096,256]{1,0:T(8,128)(2,1)} %param.14) | copy-start | bytes 6291460
  6.5 150.4 %all-reduce.3.cloned.1.call-start = ((), (), s32[]{:S(2)}) async-start(), calls=%async_computation | async-start | bytes 11534336 | tf_op jit(solution)/shard_map/psum | solution.py:91
  6.5 6.4 %slice-start = ((s8[6422528]{0:T(1024)(128)(4,1)}), s8[4194304]{0:T(1024)(128)(4,1)S(1)}, s32[]{:S(2)}) async-start(s8[6422528]{0:T(1024)(128)(4,1)} %bitcast.14), calls=%async_computation.1 | async-start | bytes 8388608
  7.4 5.6 %slice-start.1 = ((s8[6422528]{0:T(1024)(128)(4,1)}), s8[2228224]{0:T(1024)(128)(4,1)S(1)}, s32[]{:S(2)}) async-start(s8[6422528]{0:T(1024)(128)(4,1)} %bitcast.14), calls=%async_computation.2 | async-start | bytes 4456448
  13.0 3.3 %copy-start.4 = (f32[256]{0:T(256)S(1)}, f32[256]{0:T(256)}, u32[]{:S(2)}) copy-start(f32[256]{0:T(256)} %param.16) | copy-start | bytes 3076
  13.0 3.4 %copy-start.2 = (bf16[128,4096]{1,0:T(8,128)(2,1)S(1)}, bf16[128,4096]{1,0:T(8,128)(2,1)}, u32[]{:S(2)}) copy-start(bf16[128,4096]{1,0:T(8,128)(2,1)} %param.12) | copy-start | bytes 3145732
  22.0 0.7 copy-start.3
  22.0 0.9 copy-start.6
  22.0 2.3 copy-start.5
  156.9 11.1 %copy-start.1 = (bf16[512,4096]{1,0:T(8,128)(2,1)S(1)}, bf16[512,4096]{1,0:T(8,128)(2,1)}, u32[]{:S(2)}) copy-start(bf16[512,4096]{1,0:T(8,128)(2,1)} %param.18) | copy-start | bytes 12582916
Sparse Core Ops, SparseCore 0:
  22.2 134.7 all-reduce.2
where the time goes:
time: 243 us
  waiting for transfers between devices  132 us (54%)
  blocking collectives  60.4 us (25%)
  matrix products  29.1 us (12%)
  between operations  14.2 us (6%)
  other arithmetic  4.71 us (2%)
    psum x1, waiting for transfers between devices, shards(): hat = lax.psum(jnp.concatenate([part_act, part_grad], axis=1), 'wide')  132 us
    unnamed x1, blocking collectives  60.4 us
    dot_general x1, matrix products, pair_products(): lax.dot_general(hat[:, width_act:], tok_grad, inner, precision=lax.Precis...  11.1 us
    dot_general x1, matrix products, pair_products(): lax.dot_general(hat[:, :width_act], tok_act, inner, precision=lax.Precisi...  5.78 us
    dot_general x1, matrix products, shards(): jnp.dot(query_grad, basis_grad, preferred_element_type=jnp.float32)  5.59 us
  transfers between devices with their start and end apart: 1, of which 1 were waited for; matrix products, arithmetic and copies ran while one was open for 1% of the time, Pallas kernels for 0%

commit v1 on v0

v1 whole, which is shorter than its diff:
```python
import functools

import jax
import jax.numpy as jnp
from jax import lax
from jax.experimental import pallas as pl
from jax.experimental.pallas import tpu as pltpu
from jax.sharding import PartitionSpec as P

RANK = 2
DAMP = 0.1
LANES = 128
LEVELS = 32767.0
LEAST = 1e-34
MESH = pl.DeviceIdType.MESH


def remote(src, dst, send, recv, there):
    return pltpu.make_async_remote_copy(
        src_ref=src, dst_ref=dst, send_sem=send, recv_sem=recv, device_id=there, device_id_type=MESH
    )


def quantize(x):
    most = jnp.max(jnp.abs(x), axis=0, keepdims=True)
    up = jnp.where(most > LEAST, LEVELS / jnp.maximum(most, LEAST), 0.0)
    return jnp.round(x * up).astype(jnp.int32).astype(jnp.int16), most * (1.0 / LEVELS)


def dequantize(q, scale):
    return q.astype(jnp.int32).astype(jnp.float32) * scale


def reduce_kernel(
    shape,
    part_ref,
    out_ref,
    core_in,
    y_out,
    y_out_s,
    y_in,
    y_in_s,
    z_out,
    z_out_s,
    z_in,
    z_in_s,
    hat,
    hat_s,
    core_sem,
    y_sem,
    z_sem,
    az_sem,
    ay_sem,
    ac_sem,
):
    A, B, K, R, W = shape
    g = lax.axis_index("groups")
    me = lax.axis_index("wide")
    core = lax.rem(me, 2)
    b = lax.rem(me // 2, B)
    a = me // (2 * B)
    other = 1 - core
    strips = W // LANES

    def device(a_, b_, core_):
        return (g, (a_ * B + b_) * 2 + core_)

    peer = device(a, b, other)
    ys = [device(a, lax.rem(b + i, B), core) for i in range(B)]
    zs = [device(lax.rem(a + j, A), b, core) for j in range(A)]

    barrier = pltpu.get_barrier_semaphore()
    for there in [peer] + ys[1:] + zs[1:]:
        pl.semaphore_signal(barrier, inc=1, device_id=there, device_id_type=MESH)
    pl.semaphore_wait(barrier, 1 + (B - 1) + (A - 1))

    def column(core_, b_, k):
        return pl.multiple_of(((core_ * B + b_) * K + k) * W, LANES)

    def lanes(at, t):
        return pl.ds(pl.multiple_of(at + t * LANES, LANES), LANES)

    def strip_loop(body):
        def run(t, carry):
            body(t)
            return carry

        lax.fori_loop(0, strips, run, 0)

    started = []

    def go(copy):
        copy.start()
        started.append(copy)
        return copy

    def go_pair(q_src, q_dst, s_src, s_dst, sems, at, there):
        q = go(remote(q_src, q_dst, sems.at[(0, 0) + at], sems.at[(1, 0) + at], there))
        s = go(remote(s_src, s_dst, sems.at[(0, 1) + at], sems.at[(1, 1) + at], there))
        return q, s

    order = [i for i in range(1, B)] + [0]
    core_copies = {}
    for k in range(K):
        for i in order:
            bb = lax.rem(b + i, B)
            core_copies[k, i] = go(
                remote(
                    part_ref.at[:, pl.ds(column(other, bb, k), W)],
                    core_in.at[i, k],
                    core_sem.at[0, i, k],
                    core_sem.at[1, i, k],
                    peer,
                )
            )

    y_copies = {}
    for k in range(K):
        for i in range(1, B):
            at = column(core, lax.rem(b + i, B), k)
            core_copies[k, i].wait_recv()

            def send_y(t, at=at, i=i, k=k):
                q, s = quantize(part_ref[:, lanes(at, t)] + core_in[i, k, :, lanes(0, t)])
                y_out[i - 1, k, :, lanes(0, t)] = q
                y_out_s[i - 1, k, :, lanes(0, t)] = s

            strip_loop(send_y)
            y_copies[k, i] = go_pair(
                y_out.at[i - 1, k],
                y_in.at[i - 1, k],
                y_out_s.at[i - 1, k],
                y_in_s.at[i - 1, k],
                y_sem,
                (i - 1, k),
                ys[i],
            )

    z_copies = {}
    for k in range(K):
        core_copies[k, 0].wait_recv()
        for i in range(1, B):
            for c in y_copies[k, i]:
                c.wait_recv()
        at = column(core, b, k)

        def add_y(t, at=at, k=k):
            total = part_ref[:, lanes(at, t)] + core_in[0, k, :, lanes(0, t)]
            for i in range(1, B):
                total = total + dequantize(y_in[i - 1, k, :, lanes(0, t)], y_in_s[i - 1, k, :, lanes(0, t)])
            core_in[0, k, :, lanes(0, t)] = total
            for v in range(A):
                q, s = quantize(total[v * R : (v + 1) * R])
                z_out[k, v, :, lanes(0, t)] = q
                z_out_s[k, v, :, lanes(0, t)] = s

        strip_loop(add_y)
        for j in range(1, A):
            aa = lax.rem(a + j, A)
            z_copies[k, j] = go_pair(
                z_out.at[k, aa],
                z_in.at[k, j - 1],
                z_out_s.at[k, aa],
                z_in_s.at[k, j - 1],
                z_sem,
                (k, j - 1),
                zs[j],
            )

    az, ay, ac = {}, {}, {}

    def push(sems, at, there, where):
        return go_pair(hat.at[where], hat.at[where], hat_s.at[where], hat_s.at[where], sems, at, there)

    for k in range(K):
        for j in range(1, A):
            for c in z_copies[k, j]:
                c.wait_recv()
        rows = pl.ds(pl.multiple_of(a * R, R), R)

        def add_z(t, k=k, rows=rows):
            total = core_in[0, k, rows, lanes(0, t)]
            for j in range(1, A):
                total = total + dequantize(z_in[k, j - 1, :, lanes(0, t)], z_in_s[k, j - 1, :, lanes(0, t)])
            q, s = quantize(total)
            hat[core, b, k, a, :, lanes(0, t)] = q
            hat_s[core, b, k, a, :, lanes(0, t)] = s

        strip_loop(add_z)
        where = (core, b, k, a)
        for j in range(1, A):
            az[k, j] = push(az_sem, (k, j - 1), zs[j], where)
        for i in range(1, B):
            ay[k, i, 0] = push(ay_sem, (k, i - 1, 0), ys[i], where)
        ac[k, 0, 0] = push(ac_sem, (k, 0, 0), peer, where)

    for k in range(K):
        for j in range(1, A):
            for c in az[k, j]:
                c.wait_recv()
            where = (core, b, k, lax.rem(a - j + A, A))
            for i in range(1, B):
                ay[k, i, j] = push(ay_sem, (k, i - 1, j), ys[i], where)
            ac[k, 0, j] = push(ac_sem, (k, 0, j), peer, where)
        for i in range(1, B):
            for j in range(A):
                for c in ay[k, i, j]:
                    c.wait_recv()
                where = (core, lax.rem(b - i + B, B), k, lax.rem(a - j + A, A))
                ac[k, i, j] = push(ac_sem, (k, i, j), peer, where)

    for pair in ac.values():
        for c in pair:
            c.wait_recv()

    half = out_ref.shape[0] // 2
    for h in range(2):
        for bb in range(B):
            for k in range(K):

                def unpack(t, h=h, bb=bb, k=k):
                    at = lanes(((h * B + bb) * K + k) * W, t)
                    for v in range(A):
                        value = dequantize(hat[h, bb, k, v, :, lanes(0, t)], hat_s[h, bb, k, v, :, lanes(0, t)])
                        high = value.astype(jnp.bfloat16)
                        out_ref[v * R : (v + 1) * R, at] = high
                        out_ref[half + v * R : half + (v + 1) * R, at] = (
                            value - high.astype(jnp.float32)
                        ).astype(jnp.bfloat16)

                strip_loop(unpack)

    for c in started:
        c.wait_send()


def sum_everywhere(part, n):
    rows, columns = part.shape
    B = 2 if n <= 16 else 4
    A = n // (2 * B)
    R = rows // A
    tiles = columns // (2 * B * LANES)
    K = 2 if tiles % 2 == 0 else 1
    W = columns // (2 * B * K)
    f32, i16 = jnp.float32, jnp.int16
    dma = pltpu.SemaphoreType.DMA
    return pl.pallas_call(
        functools.partial(reduce_kernel, (A, B, K, R, W)),
        out_shape=jax.ShapeDtypeStruct((2 * rows, columns), jnp.bfloat16),
        in_specs=[pl.BlockSpec(memory_space=pltpu.VMEM)],
        out_specs=pl.BlockSpec(memory_space=pltpu.VMEM),
        scratch_shapes=[
            pltpu.VMEM((B, K, rows, W), f32),
            pltpu.VMEM((B - 1, K, rows, W), i16),
            pltpu.VMEM((B - 1, K, 1, W), f32),
            pltpu.VMEM((B - 1, K, rows, W), i16),
            pltpu.VMEM((B - 1, K, 1, W), f32),
            pltpu.VMEM((K, A, R, W), i16),
            pltpu.VMEM((K, A, 1, W), f32),
            pltpu.VMEM((K, A - 1, R, W), i16),
            pltpu.VMEM((K, A - 1, 1, W), f32),
            pltpu.VMEM((2, B, K, A, R, W), i16),
            pltpu.VMEM((2, B, K, A, 1, W), f32),
            dma((2, B, K)),
            dma((2, 2, B - 1, K)),
            dma((2, 2, K, A - 1)),
            dma((2, 2, K, A - 1)),
            dma((2, 2, K, B - 1, A)),
            dma((2, 2, K, B, A)),
        ],
        compiler_params=pltpu.CompilerParams(
            collective_id=0, has_side_effects=True, vmem_limit_bytes=48 * 1024 * 1024
        ),
    )(part)


def share_kernel(n, mine_ref, owner_ref, out_ref, every, send_sem, recv_sem):
    g = lax.axis_index("groups")
    me = lax.axis_index("wide")
    docs = mine_ref.shape[0]
    barrier = pltpu.get_barrier_semaphore()

    def greet(j, carry):
        pl.semaphore_signal(barrier, inc=1, device_id=(g, lax.rem(me + j, n)), device_id_type=MESH)
        return carry

    lax.fori_loop(1, n, greet, 0)
    pl.semaphore_wait(barrier, n - 1)
    every[me] = mine_ref[...]

    def copy(j):
        return remote(
            mine_ref, every.at[me], send_sem.at[j - 1], recv_sem.at[j - 1], (g, lax.rem(me + j, n))
        )

    def start(j, carry):
        copy(j).start()
        return carry

    def finish(j, carry):
        copy(j).wait()
        return carry

    lax.fori_loop(1, n, start, 0)
    lax.fori_loop(1, n, finish, 0)
    table = every[...].reshape(n * docs, mine_ref.shape[1])
    row = lax.broadcasted_iota(jnp.int32, (docs, n * docs), 0) + me * docs
    pick = (row == owner_ref[...]).astype(jnp.float32)
    out_ref[...] = jnp.dot(
        pick, table, precision=lax.Precision.HIGHEST, preferred_element_type=jnp.float32
    )


def share(mine, owners, n):
    docs, queries = mine.shape
    return pl.pallas_call(
        functools.partial(share_kernel, n),
        out_shape=jax.ShapeDtypeStruct((docs, queries), jnp.float32),
        in_specs=[pl.BlockSpec(memory_space=pltpu.VMEM)] * 2,
        out_specs=pl.BlockSpec(memory_space=pltpu.VMEM),
        scratch_shapes=[
            pltpu.VMEM((n, docs, queries), jnp.float32),
            pltpu.SemaphoreType.DMA((n - 1,)),
            pltpu.SemaphoreType.DMA((n - 1,)),
        ],
        compiler_params=pltpu.CompilerParams(collective_id=1, has_side_effects=True),
    )(mine, owners)


def split(x):
    high = lax.reduce_precision(x, 8, 7)
    return jnp.concatenate([high, x - high], axis=0).astype(jnp.bfloat16)


def joined(stacked):
    half = stacked.shape[0] // 2
    return stacked[:half] + stacked[half:]


def partial_hat(query, basis, eig, size):
    coords = jnp.dot(query, basis, preferred_element_type=jnp.float32) * (1.0 / (eig + DAMP)) * (1.0 / size)
    back = (((1,), (1,)), ((), ()))
    return joined(lax.dot_general(split(coords), basis, back, preferred_element_type=jnp.float32))


def row_size(query):
    most = jnp.max(jnp.abs(query), axis=1, keepdims=True).astype(jnp.float32)
    return jnp.where(most > 0, most, 1.0)


def shards(
    doc_len,
    doc_owner,
    query_act,
    query_grad,
    basis_act,
    basis_grad,
    eig_act,
    eig_grad,
    token_act,
    token_grad,
):
    n = lax.axis_size("wide")
    me = lax.axis_index("wide")
    width_act = query_act.shape[1]
    size_act, size_grad = row_size(query_act), row_size(query_grad)
    part = jnp.concatenate(
        [
            partial_hat(query_act, basis_act, eig_act, size_act),
            partial_hat(query_grad, basis_grad, eig_grad, size_grad),
        ],
        axis=1,
    )
    hat = sum_everywhere(part, n)

    docs = doc_len.shape[0] // n
    lengths = lax.dynamic_slice(doc_len, (me * docs,), (docs,))
    ends = jnp.sum(jnp.where(jnp.arange(docs)[:, None] >= jnp.arange(docs)[None, :], lengths[None, :], 0), axis=1)
    place = jnp.arange(token_act.shape[0])
    inside = (place[None, :] < ends[:, None]) & (place[None, :] >= (ends - lengths)[:, None])
    member = jnp.where(inside, (1.0 / lengths.astype(jnp.float32))[:, None], 0.0)

    inner = (((1,), (1,)), ((), ()))
    prod_act = joined(
        lax.dot_general(hat[:, :width_act], token_act, inner, preferred_element_type=jnp.float32)
    )
    prod_grad = joined(
        lax.dot_general(hat[:, width_act:], token_grad, inner, preferred_element_type=jnp.float32)
    )
    products = (prod_act * size_act) * (prod_grad * size_grad)
    scores = products.reshape(-1, RANK, products.shape[1]).sum(axis=1)
    mine = lax.dot_general(
        member, scores, inner, precision=lax.Precision.HIGHEST, preferred_element_type=jnp.float32
    )
    return share(mine, doc_owner[None, :], n)


def solution(mesh):
    placed = (
        P("groups"),
        P("groups"),
        P("groups", None),
        P("groups", None),
        P("groups", "wide"),
        P("groups", "wide"),
        P(("groups", "wide")),
        P(("groups", "wide")),
        P(("groups", "wide"), None),
        P(("groups", "wide"), None),
    )
    return jax.shard_map(
        shards, mesh=mesh, in_specs=placed, out_specs=P(("groups", "wide"), None), check_vma=False
    )
```

time: 243 us -> 102 us (0.42)
  waiting for transfers between devices: 132 us -> 0 us
  Pallas kernels: 0 us -> 77.2 us
  blocking collectives: 60.4 us -> 0 us
  matrix products: 29.1 us -> 13.3 us
  between operations: 14.2 us -> 0.22 us
  other arithmetic: 4.71 us -> 8.98 us
    psum x1 -> x0, waiting for transfers between devices: 132 us -> none  [shards(): hat = lax.psum(jnp.concatenate([part_act, part_grad], axis=1), 'wide')]
    pallas_call x0 -> x2, Pallas kernels: none -> 77.2 us  [the longest x1 66.5 us: sum_everywhere(): pl.pallas_call(functools.partial(reduce_kernel, (A, B, K, R, W)), out_sha...]
    unnamed x1 -> x0, blocking collectives: 60.4 us -> none
    dot_general x7, matrix products: 29.1 us -> 13.3 us  [the longest x2 6.1 us: partial_hat(): jnp.dot(query, basis, preferred_element_type=jnp.float32)]
    reduce_max x0 -> x2, other arithmetic: none -> 3.53 us  [row_size(): most = jnp.max(jnp.abs(query), axis=1, keepdims=True).astype(jnp.float32)]
  transfers between devices with their start and end apart: 1 -> 0, of which waited for: 1 -> 0; matrix products, arithmetic and copies ran while one was open for 1% -> 0% of each run, Pallas kernels for 0% -> 0%
where the time goes in v1:
time: 102 us
  Pallas kernels  77.2 us (76%)
  matrix products  13.3 us (13%)
  other arithmetic  8.98 us (9%)
  local copies, waits for them, and re-layouts  2.23 us (2%)
    pallas_call x1, Pallas kernels, sum_everywhere(): pl.pallas_call(functools.partial(reduce_kernel, (A, B, K, R, W)), out_sha...  66.5 us
    pallas_call x1, Pallas kernels, share(): pl.pallas_call(functools.partial(share_kernel, n), out_shape=jax.ShapeDty...  10.7 us
    dot_general x2, matrix products, partial_hat(): jnp.dot(query, basis, preferred_element_type=jnp.float32)  6.1 us
    reduce_max x2, other arithmetic, row_size(): most = jnp.max(jnp.abs(query), axis=1, keepdims=True).astype(jnp.float32)  3.53 us
    concatenate x1, other arithmetic, shards(): jnp.concatenate([partial_hat(query_act, basis_act, eig_act, size_act), pa...  3.33 us
    dot_general x2, matrix products, partial_hat(): lax.dot_general(split(coords), basis, back, preferred_element_type=jnp.fl...  2.84 us
    dot_general x1, matrix products, shards(): lax.dot_general(hat[:, width_act:], token_grad, inner, preferred_element_...  2.17 us
    unnamed x19, local copies, waits for them, and re-layouts  2.09 us

profile of v1, /device:TPU:0, one launch (start us, length us, event | category | flops | bytes accessed | tf_op | source)
XLA Modules:
  0.0 101.9 jit_solution(2317597884339278005)
XLA Ops:
  0.0 2.0 %abs_reduce_fusion = bf16[128]{0:T(256)(128)(2,1)S(1)} fusion(bf16[128,7168]{1,0:T(8,128)(2,1)} %param.13), kind=kLoop, calls=%fused_computation.7 | loop fusion | flops 1834880 | bytes 1835264 | tf_op jit(solution)/shard_map/reduce_max | solution.py:347
  2.0 1.5 %abs_reduce_fusion.1 = bf16[128]{0:T(256)(128)(2,1)S(1)} fusion(bf16[128,4096]{1,0:T(8,128)(2,1)} %param.12), kind=kLoop, calls=%fused_computation.12 | loop fusion | flops 1048448 | bytes 1048832 | tf_op jit(solution)/shard_map/reduce_max | solution.py:347
  3.5 0.0 slice-start
  3.6 0.8 add_divide_fusion
  4.4 5.6 %reduce-precision_convert_fusion = (bf16[128,448]{0,1:T(8,128)(2,1)S(1)}, bf16[128,448]{0,1:T(8,128)(2,1)S(1)}) fusion(f32[128]{0:T(128)S(1)} %get-tuple-element.14, f32[448]{0:T(512)S(1)} %add_divide_fusion, bf16[128,7168]{1,0:T(8,128)(2,1)} %param.13, bf16[7168,448]{0,1:T(8,128)(2,1)} %param.15), kind=kOutput, calls=%fused_computation.14 | convolution fusion | flops 822427648 | bytes 8489216 | tf_op jit(solution)/shard_map/dot_general | solution.py:341
  10.1 2.1 %fusion.10 = f32[256,7168]{1,0:T(8,128)S(1)} fusion(bf16[7168,448]{0,1:T(8,128)(2,1)S(1)} %bitcast.11, bf16[128,448]{0,1:T(8,128)(2,1)S(1)} %get-tuple-element.8, bf16[128,448]{0,1:T(8,128)(2,1)S(1)} %get-tuple-element.7), kind=kOutput, calls=%fused_computation.21 | convolution fusion | flops 1644625920 | bytes 13991936 | tf_op jit(solution)/shard_map/dot_general | solution.py:343
  12.2 0.4 slice_add_fusion
  12.6 0.2 copy-done.2
  12.9 0.6 copy-done.1
  13.4 0.5 reduce-precision_convert_fusion.1
  13.9 0.7 fusion.15
  14.6 0.2 slice_add_fusion.1
  14.9 3.3 %pad_maximum_fusion.part_ref = f32[128,11264]{1,0:T(8,128)} fusion(f32[128,7168]{1,0:T(8,128)S(1)} %slice_add_fusion, f32[128,4096]{1,0:T(8,128)S(1)} %slice_add_fusion.1), kind=kLoop, calls=%fused_computation | loop fusion | flops 1441792 | bytes 11534336 | tf_op jit(solution)/shard_map/concatenate | solution.py:367
  18.2 66.5 %shard_map.100 = bf16[256,11264]{1,0:T(8,128)(2,1)S(1)} custom-call(f32[128,11264]{1,0:T(8,128)} %pad_maximum_fusion.part_ref), custom_call_target="tpu_custom_call" | custom-call | tf_op jit(solution)/shard_map/pallas_call | solution.py:247
  84.7 2.2 %fusion = f32[256,512]{1,0:T(8,128)S(1)} fusion(bf16[512,7168]{1,0:T(8,128)(2,1)S(1)} %bitcast.14, bf16[256,11264]{1,0:T(8,128)(2,1)S(1)} %shard_map.100), kind=kOutput, calls=%fused_computation.2 | convolution fusion | flops 1879048192 | bytes 11534336 | tf_op jit(solution)/shard_map/dot_general | solution.py:388
  86.9 1.3 %fusion.2 = f32[256,512]{1,0:T(8,128)S(1)} fusion(bf16[512,4096]{1,0:T(8,128)(2,1)S(1)} %copy-done.4, bf16[256,11264]{1,0:T(8,128)(2,1)S(1)} %shard_map.100), kind=kOutput, calls=%fused_computation.5 | convolution fusion | flops 1073741824 | bytes 6815744 | tf_op jit(solution)/shard_map/dot_general | solution.py:385
  88.2 0.1 fusion.7
  88.3 0.1 reshape.33
  88.5 0.3 reduce_sum.19
  88.8 0.1 convert_divide_fusion
  88.9 0.1 select_reduce_fusion
  89.0 0.9 fusion.19.mine_ref
  89.9 10.7 %shard_map.101 = f32[8,64]{1,0:T(8,128)} custom-call(f32[8,64]{1,0:T(8,128)} %fusion.19.mine_ref, s32[1,128]{1,0:T(1,128)} %bitcast.12), custom_call_target="tpu_custom_call" | custom-call | tf_op jit(solution)/shard_map/pallas_call | solution.py:316
  100.6 1.3 %copy.12 = f32[8,64]{1,0:T(8,128)} copy(f32[8,64]{1,0:T(8,128)} %shard_map.101) | data formatting | bytes 4096
  (20 shorter events, 0.1 us)
Async XLA Ops:
  0.0 12.9 %copy-start = (bf16[4096,256]{1,0:T(8,128)(2,1)S(1)}, bf16[4096,256]{1,0:T(8,128)(2,1)}, u32[]{:S(2)}) copy-start(bf16[4096,256]{1,0:T(8,128)(2,1)} %param.14) | copy-start | bytes 6291460
  3.5 6.5 %slice-start = ((s8[6422528]{0:T(1024)(128)(4,1)}), s8[4194304]{0:T(1024)(128)(4,1)S(1)}, s32[]{:S(2)}) async-start(s8[6422528]{0:T(1024)(128)(4,1)} %bitcast.10), calls=%async_computation | async-start | bytes 8388608
  4.4 5.7 %slice-start.1 = ((s8[6422528]{0:T(1024)(128)(4,1)}), s8[2228224]{0:T(1024)(128)(4,1)S(1)}, s32[]{:S(2)}) async-start(s8[6422528]{0:T(1024)(128)(4,1)} %bitcast.10), calls=%async_computation.1 | async-start | bytes 4456448
  12.2 0.7 copy-start.2
  12.2 1.2 %copy-start.1 = (bf16[128,4096]{1,0:T(8,128)(2,1)S(1)}, bf16[128,4096]{1,0:T(8,128)(2,1)}, u32[]{:S(2)}) copy-start(bf16[128,4096]{1,0:T(8,128)(2,1)} %param.12) | copy-start | bytes 3145732
  14.9 69.8 %slice-start.2 = ((s8[7340032]{0:T(1024)(128)(4,1)}), s8[4194304]{0:T(1024)(128)(4,1)S(1)}, s32[]{:S(2)}) async-start(s8[7340032]{0:T(1024)(128)(4,1)} %bitcast.13), calls=%async_computation.2 | async-start | bytes 8388608
  18.2 66.5 %slice-start.3 = ((s8[7340032]{0:T(1024)(128)(4,1)}), s8[3145728]{0:T(1024)(128)(4,1)S(1)}, s32[]{:S(2)}) async-start(s8[7340032]{0:T(1024)(128)(4,1)} %bitcast.13), calls=%async_computation.3 | async-start | bytes 6291456
  84.7 2.2 %copy-start.4 = (bf16[512,4096]{1,0:T(8,128)(2,1)S(1)}, bf16[512,4096]{1,0:T(8,128)(2,1)}, u32[]{:S(2)}) copy-start(bf16[512,4096]{1,0:T(8,128)(2,1)} %param.18) | copy-start | bytes 12582916
  86.9 1.9 %copy-start.3 = (s32[128]{0:T(128)S(1)}, s32[128]{0:T(128)}, u32[]{:S(2)}) copy-start(s32[128]{0:T(128)} %param.10) | copy-start | bytes 1540

commit v2 on v0

v2 whole, which is shorter than its diff:
```python
import functools

import jax
import jax.numpy as jnp
from jax import lax
from jax.experimental import pallas as pl
from jax.experimental.pallas import tpu as pltpu
from jax.sharding import PartitionSpec as P

RANK = 2
DAMP = 0.1
LANES = 128
LEVELS = 32767.0
LEAST = 1e-34
PIECE = 1024
MOST_TILES = 4
MESH = pl.DeviceIdType.MESH


def remote(src, dst, send, recv, there):
    return pltpu.make_async_remote_copy(
        src_ref=src, dst_ref=dst, send_sem=send, recv_sem=recv, device_id=there, device_id_type=MESH
    )


def quantize(x):
    most = jnp.max(jnp.abs(x), axis=0, keepdims=True)
    up = jnp.where(most > LEAST, LEVELS / jnp.maximum(most, LEAST), 0.0)
    return jnp.round(x * up).astype(jnp.int32).astype(jnp.int16), most * (1.0 / LEVELS)


def dequantize(q, scale):
    return q.astype(jnp.int32).astype(jnp.float32) * scale


def chunks_of(tiles_act, tiles_grad, most):
    chunks, lane = [], 0
    for kind, tiles in ((0, tiles_act), (1, tiles_grad)):
        pieces = -(-tiles // most)
        sizes = [tiles // pieces + (1 if p < tiles % pieces else 0) for p in range(pieces)]
        offset = 0
        for size in sizes:
            chunks.append((kind, offset * LANES, lane * LANES, size * LANES))
            offset += size
            lane += size
    return chunks


def kernel(
    shape,
    chunks,
    len_ref,
    owner_ref,
    eig_act_ref,
    eig_grad_ref,
    query_act_hbm,
    query_grad_hbm,
    basis_act_hbm,
    basis_grad_hbm,
    token_act_hbm,
    token_grad_hbm,
    out_ref,
    query_act,
    query_grad,
    basis_act,
    basis_grad,
    token_act,
    token_grad,
    coords_act,
    coords_grad,
    part,
    core_in,
    y_out,
    y_out_s,
    y_in,
    y_in_s,
    z_out,
    z_out_s,
    z_in,
    z_in_s,
    hat,
    hat_s,
    prods,
    mine,
    every,
    load_sem,
    basis_sem,
    core_sem,
    y_sem,
    z_sem,
    az_sem,
    ay_sem,
    ac_sem,
    share_sem,
):
    n, A, B, R = shape
    K = len(chunks)
    rows = A * R
    f32, bf16 = jnp.float32, jnp.bfloat16
    g = lax.axis_index("groups")
    me = lax.axis_index("wide")
    core = lax.rem(me, 2)
    b = lax.rem(me // 2, B)
    a = me // (2 * B)
    other = 1 - core
    queries = (query_act, query_grad)
    bases = (basis_act, basis_grad)
    tokens = (token_act, token_grad)
    coords = (coords_act, coords_grad)
    eigs = (eig_act_ref, eig_grad_ref)

    loads = []
    for at, (src, dst) in enumerate(((query_act_hbm, query_act), (query_grad_hbm, query_grad))):
        loads.append(pltpu.make_async_copy(src, dst, load_sem.at[at]))
    pieces = []
    for kind, (src, dst) in enumerate(((basis_act_hbm, basis_act), (basis_grad_hbm, basis_grad))):
        for row in range(0, src.shape[0], PIECE):
            cut = pl.ds(row, PIECE)
            copy = pltpu.make_async_copy(src.at[cut], dst.at[cut], basis_sem.at[len(pieces)])
            pieces.append((kind, row, copy))
    for at, (src, dst) in enumerate(((token_act_hbm, token_act), (token_grad_hbm, token_grad))):
        loads.append(pltpu.make_async_copy(src, dst, load_sem.at[2 + at]))
    for copy in loads[:2] + [p[2] for p in pieces] + loads[2:]:
        copy.start()

    barrier = pltpu.get_barrier_semaphore()

    def greet(j, carry):
        pl.semaphore_signal(barrier, inc=1, device_id=(g, lax.rem(me + j, n)), device_id_type=MESH)
        return carry

    lax.fori_loop(1, n, greet, 0)

    def device(a_, b_, core_):
        return (g, (a_ * B + b_) * 2 + core_)

    peer = device(a, b, other)
    ys = [device(a, lax.rem(b + i, B), core) for i in range(B)]
    zs = [device(lax.rem(a + j, A), b, core) for j in range(A)]

    def lanes(at, t):
        return pl.ds(pl.multiple_of(at + t * LANES, LANES), LANES)

    def strip_loop(strips, body):
        def run(t, carry):
            body(t)
            return carry

        lax.fori_loop(0, strips, run, 0)

    sizes = []
    for kind in range(2):
        loads[kind].wait()
        query = queries[kind]

        def most(t, carry, query=query):
            return jnp.maximum(carry, jnp.abs(query[:, lanes(0, t)].astype(f32)))

        size = lax.fori_loop(0, query.shape[1] // LANES, most, jnp.zeros((rows, LANES), f32))
        size = jnp.max(size, axis=1, keepdims=True)
        sizes.append(jnp.where(size > 0, size, 1.0))

    for kind in range(2):
        total = jnp.zeros((rows, bases[kind].shape[1]), f32)
        for at_kind, row, copy in pieces:
            if at_kind == kind:
                copy.wait()
                total = total + jnp.dot(
                    queries[kind][:, row : row + PIECE],
                    bases[kind][row : row + PIECE, :],
                    preferred_element_type=f32,
                )
        total = total * (1.0 / (eigs[kind][...] + DAMP)) * (1.0 / sizes[kind])
        high = total.astype(bf16)
        coords[kind][:rows] = high
        coords[kind][rows:] = (total - high.astype(f32)).astype(bf16)
        prods[kind] = jnp.zeros(prods.shape[1:], f32)

    pl.semaphore_wait(barrier, n - 1)
    started = []
    inner = (((1,), (1,)), ((), ()))

    def go(copy):
        copy.start()
        started.append(copy)
        return copy

    def go_pair(q_src, q_dst, s_src, s_dst, sems, at, there):
        q = go(remote(q_src, q_dst, sems.at[(0, 0) + at], sems.at[(1, 0) + at], there))
        s = go(remote(s_src, s_dst, sems.at[(0, 1) + at], sems.at[(1, 1) + at], there))
        return q, s

    def column(core_, b_, k):
        kind, offset, _, _ = chunks[k]
        share = bases[kind].shape[0] // (2 * B)
        return pl.multiple_of((core_ * B + b_) * share + offset, LANES)

    order = [i for i in range(1, B)] + [0]
    core_copies, y_copies, z_copies, az, ay, ac = {}, {}, {}, {}, {}, {}

    def make_part(k):
        kind, _, lane, w = chunks[k]
        cut = pl.ds(lane, w)
        for where, core_ in ((1, other), (0, core)):
            for i in order:
                block = bases[kind][pl.ds(column(core_, lax.rem(b + i, B), k), w), :]
                both = lax.dot_general(coords[kind][...], block, inner, preferred_element_type=f32)
                part[where, i, :, cut] = both[:rows] + both[rows:]
                if where == 1:
                    core_copies[k, i] = go(
                        remote(
                            part.at[1, i, :, cut],
                            core_in.at[i, :, cut],
                            core_sem.at[0, i, k],
                            core_sem.at[1, i, k],
                            peer,
                        )
                    )

    def send_y(k):
        _, _, lane, w = chunks[k]
        cut = pl.ds(lane, w)
        for i in range(1, B):
            core_copies[k, i].wait_recv()

            def body(t, i=i):
                at = lanes(lane, t)
                q, s = quantize(part[0, i, :, at] + core_in[i, :, at])
                y_out[i - 1, :, at] = q
                y_out_s[i - 1, :, at] = s

            strip_loop(w // LANES, body)
            y_copies[k, i] = go_pair(
                y_out.at[i - 1, :, cut],
                y_in.at[i - 1, :, cut],
                y_out_s.at[i - 1, :, cut],
                y_in_s.at[i - 1, :, cut],
                y_sem,
                (i - 1, k),
                ys[i],
            )

    def send_z(k):
        _, _, lane, w = chunks[k]
        cut = pl.ds(lane, w)
        core_copies[k, 0].wait_recv()
        for i in range(1, B):
            for c in y_copies[k, i]:
                c.wait_recv()

        def body(t):
            at = lanes(lane, t)
            total = part[0, 0, :, at] + core_in[0, :, at]
            for i in range(1, B):
                total = total + dequantize(y_in[i - 1, :, at], y_in_s[i - 1, :, at])
            core_in[0, :, at] = total
            for v in range(A):
                q, s = quantize(total[v * R : (v + 1) * R])
                z_out[v, :, at] = q
                z_out_s[v, :, at] = s

        strip_loop(w // LANES, body)
        for j in range(1, A):
            aa = lax.rem(a + j, A)
            z_copies[k, j] = go_pair(
                z_out.at[aa, :, cut],
                z_in.at[j - 1, :, cut],
                z_out_s.at[aa, :, cut],
                z_in_s.at[j - 1, :, cut],
                z_sem,
                (k, j - 1),
                zs[j],
            )

    def send_az(k):
        _, _, lane, w = chunks[k]
        cut = pl.ds(lane, w)
        for j in range(1, A):
            for c in z_copies[k, j]:
                c.wait_recv()
        own = pl.ds(pl.multiple_of(a * R, R), R)

        def body(t):
            at = lanes(lane, t)
            total = core_in[0, own, at]
            for j in range(1, A):
                total = total + dequantize(z_in[j - 1, :, at], z_in_s[j - 1, :, at])
            q, s = quantize(total)
            hat[core, b, a, :, at] = q
            hat_s[core, b, a, :, at] = s

        strip_loop(w // LANES, body)
        q, s = hat.at[core, b, a, :, cut], hat_s.at[core, b, a, :, cut]
        for j in range(1, A):
            az[k, j] = go_pair(q, q, s, s, az_sem, (k, j - 1), zs[j])

    def send_ay(k):
        _, _, lane, w = chunks[k]
        cut = pl.ds(lane, w)
        for j in range(1, A):
            for c in az[k, j]:
                c.wait_recv()
        q, s = hat.at[core, b, :, :, cut], hat_s.at[core, b, :, :, cut]
        for i in range(1, B):
            ay[k, i] = go_pair(q, q, s, s, ay_sem, (k, i - 1), ys[i])
        ac[k, 0] = go_pair(q, q, s, s, ac_sem, (k, 0), peer)

    def send_ac(k):
        _, _, lane, w = chunks[k]
        cut = pl.ds(lane, w)
        for i in range(1, B):
            for c in ay[k, i]:
                c.wait_recv()
            bb = lax.rem(b - i + B, B)
            q, s = hat.at[core, bb, :, :, cut], hat_s.at[core, bb, :, :, cut]
            ac[k, i] = go_pair(q, q, s, s, ac_sem, (k, i), peer)

    def score(k):
        kind, offset, lane, w = chunks[k]
        cut = pl.ds(lane, w)
        share = bases[kind].shape[0] // (2 * B)
        for i in range(B):
            for c in ac[k, i]:
                c.wait_recv()
        if k == 0:
            loads[2].wait()
        if kind == 1 and chunks[k - 1][0] == 0:
            loads[3].wait()
        for h in range(2):
            for bb in range(B):
                value = dequantize(hat[h, bb, :, :, cut], hat_s[h, bb, :, :, cut]).reshape(rows, w)
                high = value.astype(bf16)
                low = (value - high.astype(f32)).astype(bf16)
                start = (h * B + bb) * share + offset
                block = tokens[kind][:, start : start + w]
                prods[kind] += lax.dot_general(
                    jnp.concatenate([high, low], axis=0), block, inner, preferred_element_type=f32
                )

    stages = (make_part, send_y, send_z, send_az, send_ay, send_ac, score)
    for step in range(K + len(stages) - 1):
        for behind, stage in enumerate(stages):
            if 0 <= step - behind < K:
                stage(step - behind)

    docs = mine.shape[0]
    slots = token_act.shape[0]
    place = lax.broadcasted_iota(jnp.int32, (docs, slots), 1)
    which = lax.broadcasted_iota(jnp.int32, (docs, slots), 0)
    member = jnp.zeros((docs, slots), f32)
    begin = jnp.int32(0)
    for d in range(docs):
        length = len_ref[0, me * docs + d]
        inside = (which == d) & (place >= begin) & (place < begin + length)
        member = jnp.where(inside, 1.0 / jnp.full((docs, slots), length, jnp.int32).astype(f32), member)
        begin = begin + length
    prod = [(prods[kind, :rows] + prods[kind, rows:]) * sizes[kind] for kind in range(2)]
    exact = dict(precision=lax.Precision.HIGHEST, preferred_element_type=f32)
    by_row = lax.dot_general(member, prod[0] * prod[1], inner, **exact)
    nq = mine.shape[1]
    row = lax.broadcasted_iota(jnp.int32, (rows, nq), 0)
    first = lax.broadcasted_iota(jnp.int32, (rows, nq), 1) * RANK
    pairs = ((row >= first) & (row < first + RANK)).astype(f32)
    result = jnp.dot(by_row, pairs, **exact)
    mine[...] = result
    every[me] = result

    def copy(j):
        return remote(
            mine, every.at[me], share_sem.at[0, j - 1], share_sem.at[1, j - 1], (g, lax.rem(me + j, n))
        )

    def start(j, carry):
        copy(j).start()
        return carry

    def finish(j, carry):
        copy(j).wait()
        return carry

    lax.fori_loop(1, n, start, 0)
    for c in started:
        c.wait_send()
    lax.fori_loop(1, n, finish, 0)
    table = every[...].reshape(n * docs, nq)
    row = lax.broadcasted_iota(jnp.int32, (docs, n * docs), 0) + me * docs
    pick = (row == owner_ref[...]).astype(f32)
    out_ref[...] = jnp.dot(pick, table, **exact)


def shards(
    doc_len,
    doc_owner,
    query_act,
    query_grad,
    basis_act,
    basis_grad,
    eig_act,
    eig_grad,
    token_act,
    token_grad,
):
    n = lax.axis_size("wide")
    rows = query_act.shape[0]
    B = 2 if n <= 16 else 4
    A = n // (2 * B)
    R = rows // A
    chunks = chunks_of(
        query_act.shape[1] // (2 * B * LANES), query_grad.shape[1] // (2 * B * LANES), MOST_TILES
    )
    K = len(chunks)
    W = chunks[-1][2] + chunks[-1][3]
    docs, nq = doc_len.shape[0] // n, rows // RANK
    slots = token_act.shape[0]
    f32, i16, bf16 = jnp.float32, jnp.int16, jnp.bfloat16
    dma = pltpu.SemaphoreType.DMA
    vmem = pl.BlockSpec(memory_space=pltpu.VMEM)
    anywhere = pl.BlockSpec(memory_space=pl.ANY)
    pieces = (basis_act.shape[0] + basis_grad.shape[0]) // PIECE
    return pl.pallas_call(
        functools.partial(kernel, (n, A, B, R), chunks),
        out_shape=jax.ShapeDtypeStruct((docs, nq), f32),
        in_specs=[pl.BlockSpec(memory_space=pltpu.SMEM), vmem, vmem, vmem] + [anywhere] * 6,
        out_specs=vmem,
        scratch_shapes=[
            pltpu.VMEM(query_act.shape, bf16),
            pltpu.VMEM(query_grad.shape, bf16),
            pltpu.VMEM(basis_act.shape, bf16),
            pltpu.VMEM(basis_grad.shape, bf16),
            pltpu.VMEM(token_act.shape, bf16),
            pltpu.VMEM(token_grad.shape, bf16),
            pltpu.VMEM((2 * rows, basis_act.shape[1]), bf16),
            pltpu.VMEM((2 * rows, basis_grad.shape[1]), bf16),
            pltpu.VMEM((2, B, rows, W), f32),
            pltpu.VMEM((B, rows, W), f32),
            pltpu.VMEM((B - 1, rows, W), i16),
            pltpu.VMEM((B - 1, 1, W), f32),
            pltpu.VMEM((B - 1, rows, W), i16),
            pltpu.VMEM((B - 1, 1, W), f32),
            pltpu.VMEM((A, R, W), i16),
            pltpu.VMEM((A, 1, W), f32),
            pltpu.VMEM((A - 1, R, W), i16),
            pltpu.VMEM((A - 1, 1, W), f32),
            pltpu.VMEM((2, B, A, R, W), i16),
            pltpu.VMEM((2, B, A, 1, W), f32),
            pltpu.VMEM((2, 2 * rows, slots), f32),
            pltpu.VMEM((docs, nq), f32),
            pltpu.VMEM((n, docs, nq), f32),
            dma((4,)),
            dma((pieces,)),
            dma((2, B, K)),
            dma((2, 2, B - 1, K)),
            dma((2, 2, K, A - 1)),
            dma((2, 2, K, A - 1)),
            dma((2, 2, K, B - 1)),
            dma((2, 2, K, B)),
            dma((2, n - 1)),
        ],
        compiler_params=pltpu.CompilerParams(
            collective_id=0, has_side_effects=True, vmem_limit_bytes=56 * 1024 * 1024
        ),
    )(
        doc_len[None, :],
        doc_owner[None, :],
        eig_act[None, :],
        eig_grad[None, :],
        query_act,
        query_grad,
        basis_act,
        basis_grad,
        token_act,
        token_grad,
    )


def solution(mesh):
    placed = (
        P("groups"),
        P("groups"),
        P("groups", None),
        P("groups", None),
        P("groups", "wide"),
        P("groups", "wide"),
        P(("groups", "wide")),
        P(("groups", "wide")),
        P(("groups", "wide"), None),
        P(("groups", "wide"), None),
    )
    return jax.shard_map(
        shards, mesh=mesh, in_specs=placed, out_specs=P(("groups", "wide"), None), check_vma=False
    )
```

time: 243 us -> 80.4 us (0.33)
  waiting for transfers between devices: 132 us -> 0 us
  Pallas kernels: 0 us -> 68.6 us
  blocking collectives: 60.4 us -> 0 us
  matrix products: 29.1 us -> 0 us
  between operations: 14.2 us -> 0.01 us
  local copies, waits for them, and re-layouts: 2.07 us -> 11.4 us
  other arithmetic: 4.71 us -> 0 us
    psum x1 -> x0, waiting for transfers between devices: 132 us -> none  [shards(): hat = lax.psum(jnp.concatenate([part_act, part_grad], axis=1), 'wide')]
    pallas_call x0 -> x1, Pallas kernels: none -> 68.6 us  [shards(): pl.pallas_call(functools.partial(kernel, (n, A, B, R), chunks), out_shape...]
    unnamed x1 -> x0, blocking collectives: 60.4 us -> none
    dot_general x7 -> x0, matrix products: 29.1 us -> none  [the longest x1 11.1 us: pair_products(): lax.dot_general(hat[:, width_act:], tok_grad, inner, precision=lax.Precis...]
    unnamed x20 -> x2, local copies, waits for them, and re-layouts: 1.84 us -> 11.4 us
    concatenate x1 -> x0, other arithmetic: 2.95 us -> none  [shards(): hat = lax.psum(jnp.concatenate([part_act, part_grad], axis=1), 'wide')]
  transfers between devices with their start and end apart: 1 -> 0, of which waited for: 1 -> 0; matrix products, arithmetic and copies ran while one was open for 1% -> 0% of each run, Pallas kernels for 0% -> 0%
where the time goes in v2:
time: 80.4 us; the launch traced here: 80 us
  Pallas kernels  68.6 us (85%)
  local copies, waits for them, and re-layouts  11.4 us (14%)
    pallas_call x1, Pallas kernels, shards(): pl.pallas_call(functools.partial(kernel, (n, A, B, R), chunks), out_shape...  68.6 us
    unnamed x2, local copies, waits for them, and re-layouts  11.4 us

profile of v2, /device:TPU:0, one launch (start us, length us, event | category | flops | bytes accessed | tf_op | source)
XLA Modules:
  0.0 80.0 jit_solution(13442125914969322443)
XLA Ops:
  0.0 10.1 %copy.11.basis_grad_hbm = bf16[7168,448]{1,0:T(8,128)(2,1)} copy(bf16[7168,448]{0,1:T(8,128)(2,1)} %param.15) | data formatting | bytes 12845056 | tf_op args[5]
  10.1 68.6 %shard_map.100 = f32[8,64]{1,0:T(8,128)} custom-call(s32[1,128]{1,0:T(1,128)} %bitcast.6, s32[1,128]{1,0:T(1,128)} %bitcast.7, f32[1,256]{1,0:T(1,128)} %bitcast.5, f32[1,448]{1,0:T(1,128)} %bitcast.4, bf16[128,4096]{1,0:T(8,128)(2,1)} %query_act_hbm.1, bf16[128,7168]{1,0:T(8,128)(2,1)} %query_grad_hbm.1, bf16[4096,256]{1,0:T(8,128)(2,1)} %basis_act_hbm.1, ...), custom_call_target="tpu_custom_call" | custom-call | tf_op jit(solution)/shard_map/pallas_call | solution.py:420
  78.7 1.3 %copy.13 = f32[8,64]{1,0:T(8,128)} copy(f32[8,64]{1,0:T(8,128)} %shard_map.100) | data formatting | bytes 4096

commit v3 on v2

--- a/solution.py
+++ b/solution.py
@@ -114,14 +114,15 @@
         loads.append(pltpu.make_async_copy(src, dst, load_sem.at[at]))
     pieces = []
     for kind, (src, dst) in enumerate(((basis_act_hbm, basis_act), (basis_grad_hbm, basis_grad))):
-        for row in range(0, src.shape[0], PIECE):
-            cut = pl.ds(row, PIECE)
+        for row in range(0, src.shape[kind], PIECE):
+            cut = (pl.ds(row, PIECE), slice(None)) if kind == 0 else (slice(None), pl.ds(row, PIECE))
             copy = pltpu.make_async_copy(src.at[cut], dst.at[cut], basis_sem.at[len(pieces)])
             pieces.append((kind, row, copy))
     for at, (src, dst) in enumerate(((token_act_hbm, token_act), (token_grad_hbm, token_grad))):
         loads.append(pltpu.make_async_copy(src, dst, load_sem.at[2 + at]))
-    for copy in loads[:2] + [p[2] for p in pieces] + loads[2:]:
-        copy.start()
+    for kind in range(2):
+        for copy in [loads[kind]] + [p[2] for p in pieces if p[0] == kind]:
+            copy.start()
 
     barrier = pltpu.get_barrier_semaphore()
 
@@ -139,46 +140,42 @@
     zs = [device(lax.rem(a + j, A), b, core) for j in range(A)]
 
     def lanes(at, t):
-        return pl.ds(pl.multiple_of(at + t * LANES, LANES), LANES)
+        return pl.ds(at + t * LANES, LANES)
 
     def strip_loop(strips, body):
-        def run(t, carry):
+        for t in range(strips):
             body(t)
-            return carry
-
-        lax.fori_loop(0, strips, run, 0)
-
+
+    inner = (((1,), (1,)), ((), ()))
     sizes = []
-    for kind in range(2):
+
+    def project(kind):
         loads[kind].wait()
         query = queries[kind]
-
-        def most(t, carry, query=query):
-            return jnp.maximum(carry, jnp.abs(query[:, lanes(0, t)].astype(f32)))
-
-        size = lax.fori_loop(0, query.shape[1] // LANES, most, jnp.zeros((rows, LANES), f32))
-        size = jnp.max(size, axis=1, keepdims=True)
+        most = jnp.zeros((rows, LANES), bf16)
+        for at in range(0, query.shape[1], LANES):
+            most = jnp.maximum(most, jnp.abs(query[:, at : at + LANES]))
+        size = jnp.max(most.astype(f32), axis=1, keepdims=True)
         sizes.append(jnp.where(size > 0, size, 1.0))
-
-    for kind in range(2):
-        total = jnp.zeros((rows, bases[kind].shape[1]), f32)
+        total = jnp.zeros((rows, bases[kind].shape[1 - kind]), f32)
         for at_kind, row, copy in pieces:
             if at_kind == kind:
                 copy.wait()
-                total = total + jnp.dot(
-                    queries[kind][:, row : row + PIECE],
-                    bases[kind][row : row + PIECE, :],
-                    preferred_element_type=f32,
-                )
+                cut = slice(row, row + PIECE)
+                block = query[:, cut]
+                if kind == 0:
+                    total = total + jnp.dot(block, bases[0][cut, :], preferred_element_type=f32)
+                else:
+                    total = total + lax.dot_general(block, bases[1][:, cut], inner, preferred_element_type=f32)
         total = total * (1.0 / (eigs[kind][...] + DAMP)) * (1.0 / sizes[kind])
         high = total.astype(bf16)
         coords[kind][:rows] = high
         coords[kind][rows:] = (total - high.astype(f32)).astype(bf16)
         prods[kind] = jnp.zeros(prods.shape[1:], f32)
 
+    project(0)
     pl.semaphore_wait(barrier, n - 1)
     started = []
-    inner = (((1,), (1,)), ((), ()))
 
     def go(copy):
         copy.start()
@@ -192,7 +189,7 @@
 
     def column(core_, b_, k):
         kind, offset, _, _ = chunks[k]
-        share = bases[kind].shape[0] // (2 * B)
+        share = tokens[kind].shape[1] // (2 * B)
         return pl.multiple_of((core_ * B + b_) * share + offset, LANES)
 
     order = [i for i in range(1, B)] + [0]
@@ -201,10 +198,17 @@
     def make_part(k):
         kind, _, lane, w = chunks[k]
         cut = pl.ds(lane, w)
+        if kind == 1 and chunks[k - 1][0] == 0:
+            project(1)
+            for copy in loads[2:]:
+                copy.start()
         for where, core_ in ((1, other), (0, core)):
             for i in order:
-                block = bases[kind][pl.ds(column(core_, lax.rem(b + i, B), k), w), :]
-                both = lax.dot_general(coords[kind][...], block, inner, preferred_element_type=f32)
+                at = pl.ds(column(core_, lax.rem(b + i, B), k), w)
+                if kind == 0:
+                    both = lax.dot_general(coords[0][...], bases[0][at, :], inner, preferred_element_type=f32)
+                else:
+                    both = jnp.dot(coords[1][...], bases[1][:, at], preferred_element_type=f32)
                 part[where, i, :, cut] = both[:rows] + both[rows:]
                 if where == 1:
                     core_copies[k, i] = go(
@@ -318,7 +322,7 @@
     def score(k):
         kind, offset, lane, w = chunks[k]
         cut = pl.ds(lane, w)
-        share = bases[kind].shape[0] // (2 * B)
+        share = tokens[kind].shape[1] // (2 * B)
         for i in range(B):
             for c in ac[k, i]:
                 c.wait_recv()
@@ -416,7 +420,7 @@
     dma = pltpu.SemaphoreType.DMA
     vmem = pl.BlockSpec(memory_space=pltpu.VMEM)
     anywhere = pl.BlockSpec(memory_space=pl.ANY)
-    pieces = (basis_act.shape[0] + basis_grad.shape[0]) // PIECE
+    pieces = (query_act.shape[1] + query_grad.shape[1]) // PIECE
     return pl.pallas_call(
         functools.partial(kernel, (n, A, B, R), chunks),
         out_shape=jax.ShapeDtypeStruct((docs, nq), f32),
@@ -426,7 +430,7 @@
             pltpu.VMEM(query_act.shape, bf16),
             pltpu.VMEM(query_grad.shape, bf16),
             pltpu.VMEM(basis_act.shape, bf16),
-            pltpu.VMEM(basis_grad.shape, bf16),
+            pltpu.VMEM(basis_grad.shape[::-1], bf16),
             pltpu.VMEM(token_act.shape, bf16),
             pltpu.VMEM(token_grad.shape, bf16),
             pltpu.VMEM((2 * rows, basis_act.shape[1]), bf16),
@@ -467,7 +471,7 @@
         query_act,
         query_grad,
         basis_act,
-        basis_grad,
+        basis_grad.T,
         token_act,
         token_grad,
     )

time: 80.4 us -> 67.1 us (0.83)
  local copies, waits for them, and re-layouts: 11.4 us -> 1.28 us
  Pallas kernels: 68.6 us -> 65.6 us
    unnamed x2 -> x1, local copies, waits for them, and re-layouts: 11.4 us -> 1.28 us
    pallas_call x1, Pallas kernels: 68.6 us -> 65.6 us  [shards(): pl.pallas_call(functools.partial(kernel, (n, A, B, R), chunks), out_shape...]
where the time goes in v3:
time: 67.1 us; the launch traced here: 66.9 us
  Pallas kernels  65.6 us (98%)
  local copies, waits for them, and re-layouts  1.28 us (2%)
    pallas_call x1, Pallas kernels, shards(): pl.pallas_call(functools.partial(kernel, (n, A, B, R), chunks), out_shape...  65.6 us

profile of v3, /device:TPU:0, one launch (start us, length us, event | category | flops | bytes accessed | tf_op | source)
XLA Modules:
  0.0 66.9 jit_solution(1795876688365103358)
XLA Ops:
  0.0 65.6 %shard_map.100 = f32[8,64]{1,0:T(8,128)} custom-call(s32[1,128]{1,0:T(1,128)} %bitcast.8, s32[1,128]{1,0:T(1,128)} %bitcast.9, f32[1,256]{1,0:T(1,128)} %bitcast.7, f32[1,448]{1,0:T(1,128)} %bitcast.6, bf16[128,4096]{1,0:T(8,128)(2,1)} %query_act_hbm.1, bf16[128,7168]{1,0:T(8,128)(2,1)} %query_grad_hbm.1, bf16[4096,256]{1,0:T(8,128)(2,1)} %basis_act_hbm.1, ...), custom_call_target="tpu_custom_call" | custom-call | tf_op jit(solution)/shard_map/pallas_call | solution.py:424
  65.6 1.3 %copy.12 = f32[8,64]{1,0:T(8,128)} copy(f32[8,64]{1,0:T(8,128)} %shard_map.100) | data formatting | bytes 4096

commit v4 on v3

--- a/solution.py
+++ b/solution.py
@@ -343,7 +343,8 @@
 
     stages = (make_part, send_y, send_z, send_az, send_ay, send_ac, score)
     for step in range(K + len(stages) - 1):
-        for behind, stage in enumerate(stages):
+        for behind in (1, 0, 2, 3, 4, 5, 6):
+            stage = stages[behind]
             if 0 <= step - behind < K:
                 stage(step - behind)
 

time: 67.1 us -> 66 us (0.984)
  Pallas kernels: 65.6 us -> 64.5 us
    pallas_call x1, Pallas kernels: 65.6 us -> 64.5 us  [shards(): pl.pallas_call(functools.partial(kernel, (n, A, B, R), chunks), out_shape...]
where the time goes in v4:
time: 66 us; the launch traced here: 65.8 us
  Pallas kernels  64.5 us (98%)
  local copies, waits for them, and re-layouts  1.28 us (2%)
    pallas_call x1, Pallas kernels, shards(): pl.pallas_call(functools.partial(kernel, (n, A, B, R), chunks), out_shape...  64.5 us

profile of v4, /device:TPU:0, one launch (start us, length us, event | category | flops | bytes accessed | tf_op | source)
XLA Modules:
  0.0 65.8 jit_solution(13069542698015305341)
XLA Ops:
  0.0 64.5 %shard_map.100 = f32[8,64]{1,0:T(8,128)} custom-call(s32[1,128]{1,0:T(1,128)} %bitcast.8, s32[1,128]{1,0:T(1,128)} %bitcast.9, f32[1,256]{1,0:T(1,128)} %bitcast.7, f32[1,448]{1,0:T(1,128)} %bitcast.6, bf16[128,4096]{1,0:T(8,128)(2,1)} %query_act_hbm.1, bf16[128,7168]{1,0:T(8,128)(2,1)} %query_grad_hbm.1, bf16[4096,256]{1,0:T(8,128)(2,1)} %basis_act_hbm.1, ...), custom_call_target="tpu_custom_call" | custom-call | tf_op jit(solution)/shard_map/pallas_call | solution.py:425
  64.6 1.3 %copy.12 = f32[8,64]{1,0:T(8,128)} copy(f32[8,64]{1,0:T(8,128)} %shard_map.100) | data formatting | bytes 4096
